TPU v7x, 32 devices: a whole 2x2x4 slice. The times are simulated.
32 devices in a mesh: grp: 8 (over z, core), blk: 4 (over y, x).
Axes of the slice: x: 2, y: 2, z: 4, core: 2. Of those that a mesh axis runs over, the one named last changes fastest.
Arguments:
- solid_fraction: float32 [192, 32, 2048], P('grp', 'blk'), may hold values from 0.2 to 1
- thermal_state: float32 [192, 32, 2048], P('grp', 'blk'), may hold values from -6 to 6
- target_heat_sensitivity: float32 [192, 32, 2048], P('grp', 'blk'), may hold values from -6 to 6
- coolant_coupling: float32 [192, 32, 2048], P('grp', 'blk'), may hold values from 0.25 to 2
- design_switch: int32 [8, 4, 8], P('grp', 'blk'), may hold values from 0 to 1, as said below
Outputs:
- sensitivity: float32 [192, 32, 2048], P('grp', 'blk')
Inputs may be any that keep to these rules, and one draw needn't show every extreme that they name: `design_switch`: every device's 8 blocks hold at least one active block, and on some device all 8 are active.
All inputs are finite; a program needn't handle non-finite values.
Results may differ from a plain program's by a relative error of at most 0.0001.
Values sent between devices are 32-bit elements; how exact they have to be, the bound alone decides.
A program may use at most 128 MiB of HBM per device.

v0:
```python
import functools

import jax
import jax.numpy as jnp
from jax import lax
from jax.experimental import pallas as pl
from jax.experimental.pallas import tpu as pltpu
from jax.sharding import PartitionSpec as P

BX = 256
RADIUS = 48
SWEEPS = 4
COND_FLOOR = 0.001
REPORT_SCALE = 100.0
GROUP = 8

MESH = pl.DeviceIdType.MESH
F32 = jnp.float32


def coverage(position, length):
    low = jnp.maximum(RADIUS - position, 0)
    high = jnp.maximum(RADIUS - (length - 1 - position), 0)
    lost = low * (low + 1) // 2 + high * (high + 1) // 2
    return ((RADIUS + 1) ** 2 - lost).astype(F32)


def kernel(n_grp, n_blk, near, far, *refs):
    (
        solid_hbm, temp_hbm, target_hbm, coupling_hbm, switch,
        out,
        solid, temp, target, coupling, cond, adj, third, fixed, raw, filt,
        y_send, y_recv, mom_send, mom_recv, zmom_send, zmom_recv, far_z,
        mask, scale, z_inv, padded, cone,
        load_sem, y_ssem, y_rsem, z_ssem, z_rsem,
        mom_ssem, mom_rsem, zm_ssem, zm_rsem, fz_ssem, fz_rsem,
    ) = refs[:39]
    depth, span, extent = solid.shape
    groups = depth // GROUP
    grp = lax.axis_index("grp")
    blk = lax.axis_index("blk")
    reach = max(near + far)

    def has(axis, step):
        if axis == "grp":
            at, count = grp + step, n_grp
        else:
            at, count = blk + step, n_blk
        return (at < count) if step > 0 else (at >= 0)

    def peer(axis, step):
        return {axis: (grp if axis == "grp" else blk) + step}

    partners = [("grp", s * d) for d in (1, 2) for s in (1, -1) if d < n_grp]
    partners += [("blk", s * d) for d in near + far for s in (1, -1)]

    loads = [
        pltpu.make_async_copy(solid_hbm, solid, load_sem.at[0]),
        pltpu.make_async_copy(temp_hbm, temp.at[pl.ds(1, depth)], load_sem.at[1]),
        pltpu.make_async_copy(target_hbm, target, load_sem.at[2]),
        pltpu.make_async_copy(coupling_hbm, coupling, load_sem.at[3]),
    ]
    for load in loads:
        load.start()

    barrier = pltpu.get_barrier_semaphore()
    total = 0
    for axis, step in partners:
        total = total + has(axis, step).astype(jnp.int32)

        @pl.when(has(axis, step))
        def _(axis=axis, step=step):
            pl.semaphore_signal(
                barrier, inc=1, device_id=peer(axis, step), device_id_type=MESH
            )

    for side, step in ((0, -1), (1, 1)):
        edge = 0 if side == 0 else depth + 1

        @pl.when(jnp.logical_not(has("grp", step)))
        def _(side=side, edge=edge):
            zero = jnp.zeros((span, extent), F32)
            cond[edge] = zero
            temp[edge] = zero
            for s in range(SWEEPS + 1):
                adj[s, edge] = zero
            zmom_recv[side] = jnp.zeros((2, span, extent), F32)

        @pl.when(jnp.logical_not(has("grp", 2 * step)))
        def _(side=side):
            far_z[side] = jnp.zeros((depth, span, extent), F32)

        @pl.when(jnp.logical_not(has("blk", step)))
        def _(side=side):
            for item in range(SWEEPS + 3):
                y_recv[item, side] = jnp.zeros((depth, extent), F32)

        for k, d in enumerate(near):

            @pl.when(jnp.logical_not(has("blk", d * step)))
            def _(side=side, k=k):
                mom_recv[k, side] = jnp.zeros((2, depth, extent), F32)

        for k, d in enumerate(far):

            @pl.when(jnp.logical_not(has("blk", d * step)))
            def _(side=side, k=k):
                refs[39][k, side] = jnp.zeros((depth, span, extent), F32)

    row = lax.broadcasted_iota(jnp.int32, (span, extent), 0)
    lane = lax.broadcasted_iota(jnp.int32, (span, extent), 1)
    row_f = row.astype(F32)

    for b in range(extent // BX):
        mask[:, b * BX : (b + 1) * BX] = jnp.full(
            (span, BX), switch[0, 0, b].astype(F32), F32
        )
    scale[...] = (
        mask[...]
        * (-1.5 * (1.0 - COND_FLOOR))
        / (coverage(lane, extent) * coverage(row + blk * span, span * n_blk))
    )
    z_inv[...] = 1.0 / coverage(
        lax.broadcasted_iota(jnp.int32, (depth, extent), 0) + grp * depth, depth * n_grp
    )
    cone[...] = jnp.maximum(
        RADIUS
        + 1
        - jnp.abs(
            lax.broadcasted_iota(jnp.int32, (2 * BX, BX), 0)
            - BX // 2
            - lax.broadcasted_iota(jnp.int32, (2 * BX, BX), 1)
        ),
        0,
    ).astype(F32).astype(jnp.bfloat16)
    padded[:, :, : BX // 2] = jnp.zeros((depth, span, BX // 2), F32)
    padded[:, :, extent + BX // 2 :] = jnp.zeros((depth, span, BX // 2), F32)

    def remote(src, dst, ssem, rsem, axis, step):
        return pltpu.make_async_remote_copy(
            src_ref=src, dst_ref=dst, send_sem=ssem, recv_sem=rsem,
            device_id=peer(axis, step), device_id_type=MESH,
        )

    def y_copy(item, g, side):
        rows = pl.ds(g * GROUP, GROUP)
        return remote(
            y_send.at[item, side, rows], y_recv.at[item, side, rows],
            y_ssem.at[item, g, side], y_rsem.at[item, g, side],
            "blk", 1 if side == 0 else -1,
        )

    def z_copy(item, buf, side):
        src, dst = (depth, 0) if side == 0 else (1, depth + 1)
        return remote(
            buf.at[src], buf.at[dst], z_ssem.at[item, side], z_rsem.at[item, side],
            "grp", 1 if side == 0 else -1,
        )

    def mom_copy(k, g, side):
        rows = pl.ds(g * GROUP, GROUP)
        return remote(
            mom_send.at[:, rows], mom_recv.at[k, side, :, rows],
            mom_ssem.at[k, g, side], mom_rsem.at[k, g, side],
            "blk", near[k] if side == 0 else -near[k],
        )

    def far_y_copy(k, g, side):
        rows = pl.ds(g * GROUP, GROUP)
        return remote(
            raw.at[rows], refs[39].at[k, side, rows],
            refs[40].at[k, g, side], refs[41].at[k, g, side],
            "blk", far[k] if side == 0 else -far[k],
        )

    def far_z_copy(g, side):
        rows = pl.ds(g * GROUP, GROUP)
        return remote(
            filt.at[rows], far_z.at[side, rows], fz_ssem.at[g, side], fz_rsem.at[g, side],
            "grp", 2 if side == 0 else -2,
        )

    def zmom_copy(side):
        return remote(
            zmom_send, zmom_recv.at[side], zm_ssem.at[side], zm_rsem.at[side],
            "grp", 1 if side == 0 else -1,
        )

    def both(make, axis, step, act):
        for side, sign in ((0, 1), (1, -1)):
            where = has(axis, -sign * step) if act == "come" else has(axis, sign * step)

            @pl.when(where)
            def _(side=side):
                copy = make(side)
                if act == "start":
                    copy.start()
                elif act == "sent":
                    copy.wait_send()
                else:
                    copy.wait_recv()

    def one(make, axis, step, side, act):
        sign = 1 if side == 0 else -1
        where = has(axis, -sign * step) if act == "come" else has(axis, sign * step)

        @pl.when(where)
        def _():
            copy = make(side)
            if act == "start":
                copy.start()
            elif act == "sent":
                copy.wait_send()
            else:
                copy.wait_recv()

    def x_shift(v):
        low = jnp.where(lane == 0, 0.0, pltpu.roll(v, 1, 1))
        high = jnp.where(lane == extent - 1, 0.0, pltpu.roll(v, extent - 1, 1))
        return low, high

    def y_shift(v, low_row, high_row):
        low = jnp.where(row == 0, low_row, pltpu.roll(v, 1, 0))
        high = jnp.where(row == span - 1, high_row, pltpu.roll(v, span - 1, 0))
        return low, high

    def halo(item, z):
        return y_recv[item, 0, pl.ds(z, 1), :], y_recv[item, 1, pl.ds(z, 1), :]

    def put_rows(item, z, v):
        y_send[item, 0, pl.ds(z, 1), :] = v[span - 1 : span]
        y_send[item, 1, pl.ds(z, 1), :] = v[0:1]

    def layers(g, body):
        @pl.loop(g * GROUP, (g + 1) * GROUP)
        def _(z):
            body(z)

    loads[0].wait()
    loads[1].wait()

    def conductivity(z):
        s = solid[z]
        c = COND_FLOOR + (1.0 - COND_FLOOR) * (s * s * s)
        cond[z + 1] = c
        put_rows(0, z, c)
        put_rows(1, z, temp[z + 1])

    pl.semaphore_wait(barrier, total)
    for g in range(groups):
        layers(g, conductivity)
        both(functools.partial(y_copy, 0, g), "blk", 1, "start")
        if g == 0:
            one(functools.partial(z_copy, 0, cond), "grp", 1, 1, "start")
    one(functools.partial(z_copy, 0, cond), "grp", 1, 0, "start")
    loads[2].wait()
    loads[3].wait()

    def start_adjoint(z):
        c = cond[z + 1]
        low_row, high_row = halo(0, z)
        xl, xh = x_shift(c)
        yl, yh = y_shift(c, low_row, high_row)
        near_sum = (cond[z] + cond[z + 2]) + (xl + xh) + (yl + yh)
        inverse = 1.0 / (coupling[z] + 3.0 * c + 0.5 * near_sum)
        a = target[z] * inverse
        third[z] = inverse * (1.0 / 3.0)
        fixed[z] = a * (2.0 / 3.0)
        adj[0, z + 1] = a
        put_rows(2, z, a)

    def sweep(s, z):
        c = cond[z + 1]
        a = adj[s, z + 1]
        cl, ch = halo(0, z)
        al, ah = halo(s + 2, z)
        ca = c * a
        axl, axh = x_shift(a)
        gxl, gxh = x_shift(ca)
        ayl, ayh = y_shift(a, al, ah)
        gyl, gyh = y_shift(ca, cl * al, ch * ah)
        below, above = adj[s, z], adj[s, z + 2]
        plain = (below + above) + (axl + axh) + (ayl + ayh)
        weighted = (cond[z] * below + cond[z + 2] * above) + (gxl + gxh) + (gyl + gyh)
        new = a * (1.0 / 3.0) + fixed[z] + third[z] * (c * plain + weighted)
        adj[s + 1, z + 1] = new
        put_rows(s + 3, z, new)

    def raw_terms(z):
        a = adj[SWEEPS, z + 1]
        t = temp[z + 1]
        al, ah = halo(SWEEPS + 2, z)
        tl, th = halo(1, z)
        axl, axh = x_shift(a)
        txl, txh = x_shift(t)
        ayl, ayh = y_shift(a, al, ah)
        tyl, tyh = y_shift(t, tl, th)
        total_terms = (
            (a - adj[SWEEPS, z]) * (t - temp[z])
            + (a - adj[SWEEPS, z + 2]) * (t - temp[z + 2])
            + (a - axl) * (t - txl)
            + (a - axh) * (t - txh)
            + (a - ayl) * (t - tyl)
            + (a - ayh) * (t - tyh)
        )
        s = solid[z]
        value = total_terms * (s * s) * scale[...] * z_inv[pl.ds(z, 1), :]
        raw[z] = value
        mom_send[0, pl.ds(z, 1), :] = jnp.sum(value, axis=0, keepdims=True)
        mom_send[1, pl.ds(z, 1), :] = jnp.sum(value * row_f, axis=0, keepdims=True)

    def stage(item, buf, body, wait_item, wait_buf, after):
        for g in range(groups):
            both(functools.partial(y_copy, wait_item, g), "blk", 1, "come")
            if wait_item == SWEEPS + 2:
                both(functools.partial(y_copy, 1, g), "blk", 1, "come")
            if g == 0:
                one(functools.partial(z_copy, wait_item, wait_buf), "grp", 1, 0, "come")
                if wait_item == SWEEPS + 2:
                    one(functools.partial(z_copy, 1, temp), "grp", 1, 0, "come")
            if g == groups - 1:
                one(functools.partial(z_copy, wait_item, wait_buf), "grp", 1, 1, "come")
                if wait_item == SWEEPS + 2:
                    one(functools.partial(z_copy, 1, temp), "grp", 1, 1, "come")
            layers(g, body)
            if item is None:
                after(g)
            else:
                both(functools.partial(y_copy, item, g), "blk", 1, "start")
                if g == 0:
                    one(functools.partial(z_copy, item, buf), "grp", 1, 1, "start")
        if item is not None:
            one(functools.partial(z_copy, item, buf), "grp", 1, 0, "start")

    stage(2, adj.at[0], start_adjoint, 0, cond, None)
    for g in range(groups):
        both(functools.partial(y_copy, 1, g), "blk", 1, "start")
    both(functools.partial(z_copy, 1, temp), "grp", 1, "start")
    for s in range(SWEEPS):
        stage(s + 3, adj.at[s + 1], functools.partial(sweep, s), s + 2, adj.at[s], None)

    def send_moments(g):
        for k, d in enumerate(near):
            both(functools.partial(mom_copy, k, g), "blk", d, "start")
        for k, d in enumerate(far):
            both(functools.partial(far_y_copy, k, g), "blk", d, "start")

    stage(None, None, raw_terms, SWEEPS + 2, adj.at[SWEEPS], send_moments)

    zmom_send[...] = jnp.zeros((2, span, extent), F32)

    def along_y(z):
        level = jnp.zeros((1, extent), F32)
        slope = jnp.zeros((1, extent), F32)
        for k, d in enumerate(near):
            weight = float(RADIUS + 1 - span * d)
            low0, low1 = mom_recv[k, 0, 0, pl.ds(z, 1), :], mom_recv[k, 0, 1, pl.ds(z, 1), :]
            high0, high1 = mom_recv[k, 1, 0, pl.ds(z, 1), :], mom_recv[k, 1, 1, pl.ds(z, 1), :]
            level = level + weight * (low0 + high0) + (low1 - high1)
            slope = slope + (high0 - low0)
        value = level + slope * row_f
        here = raw[z]
        for i in range(span):
            value = value + (RADIUS + 1 - jnp.abs(row - i)).astype(F32) * here[i : i + 1]
        for k, d in enumerate(far):
            low, high = refs[39][k, 0, z], refs[39][k, 1, z]
            for i in range(span):
                w_low = jnp.maximum(RADIUS + 1 - (span * d + row - i), 0).astype(F32)
                w_high = jnp.maximum(RADIUS + 1 - (span * d + i - row), 0).astype(F32)
                value = value + w_low * low[i : i + 1] + w_high * high[i : i + 1]
        filt[z] = value
        zmom_send[0] += value
        zmom_send[1] += value * jnp.asarray(z, F32)

    for g in range(groups):
        for k, d in enumerate(near):
            both(functools.partial(mom_copy, k, g), "blk", d, "come")
        for k, d in enumerate(far):
            both(functools.partial(far_y_copy, k, g), "blk", d, "come")
        layers(g, along_y)
        both(functools.partial(far_z_copy, g), "grp", 2, "start")
    both(zmom_copy, "grp", 1, "start")
    both(zmom_copy, "grp", 1, "come")
    for g in range(groups):
        both(functools.partial(far_z_copy, g), "grp", 2, "come")

    width = 512

    @pl.loop(0, extent // width)
    def _(b):
        cols = pl.ds(pl.multiple_of(b * width, width), width)
        shifted = pl.ds(pl.multiple_of(b * width + BX // 2, 128), width)
        own0, own1 = zmom_send[0, :, cols], zmom_send[1, :, cols]
        low0, low1 = zmom_recv[0, 0, :, cols], zmom_recv[0, 1, :, cols]
        high0, high1 = zmom_recv[1, 0, :, cols], zmom_recv[1, 1, :, cols]
        weight = float(RADIUS + 1 - depth)
        level = (RADIUS + 1.0) * own0 - own1 + weight * (low0 + high0) + low1 - high1
        slope = own0 - low0 + high0
        zero = jnp.zeros((span, width), F32)

        def up(z, carry):
            line, twice, once, far_twice, far_once = carry
            far_once = far_once + far_z[1, z, :, cols]
            far_twice = far_twice + far_once
            padded[z, :, shifted] = line - 2.0 * twice + far_twice
            once = once + filt[z, :, cols]
            return line + slope, twice + once, once, far_twice, far_once

        lax.fori_loop(0, depth, up, (level, zero, zero, zero, zero))

        def down(k, carry):
            far_twice, far_once = carry
            z = depth - 1 - k
            far_once = far_once + far_z[0, z, :, cols]
            far_twice = far_twice + far_once
            padded[z, :, shifted] += far_twice
            return far_twice, far_once

        lax.fori_loop(0, depth, down, (zero, zero))

    @pl.loop(0, extent // BX)
    def _(b):
        window = padded[:, :, pl.ds(pl.multiple_of(b * BX, BX), 2 * BX)]
        window = window.reshape(depth * span, 2 * BX)
        high = window.astype(jnp.bfloat16)
        low = (window - high.astype(F32)).astype(jnp.bfloat16)
        weights = cone[...]
        product = jnp.dot(high, weights, preferred_element_type=F32) + jnp.dot(
            low, weights, preferred_element_type=F32
        )
        cols = pl.ds(pl.multiple_of(b * BX, BX), BX)
        out[:, :, cols] = product.reshape(depth, span, BX) * (
            REPORT_SCALE * mask[:, cols]
        )

    for item in range(SWEEPS + 3):
        for g in range(groups):
            both(functools.partial(y_copy, item, g), "blk", 1, "sent")
        buf = (cond, temp)[item] if item < 2 else adj.at[item - 2]
        both(functools.partial(z_copy, item, buf), "grp", 1, "sent")
    for g in range(groups):
        for k, d in enumerate(near):
            both(functools.partial(mom_copy, k, g), "blk", d, "sent")
        for k, d in enumerate(far):
            both(functools.partial(far_y_copy, k, g), "blk", d, "sent")
        both(functools.partial(far_z_copy, g), "grp", 2, "sent")
    both(zmom_copy, "grp", 1, "sent")


def local(n_grp, n_blk, solid, temp, target, coupling, switch):
    depth, span, extent = solid.shape
    groups = depth // GROUP
    assert 2 * depth == RADIUS and depth % GROUP == 0
    near, far = [], []
    for d in range(1, n_blk):
        if (d + 1) * span - 1 <= RADIUS + 1:
            near.append(d)
        elif (d - 1) * span + 1 <= RADIUS:
            far.append(d)
    items = SWEEPS + 3
    block = (depth, span, extent)
    framed = (depth + 2, span, extent)
    vmem = lambda *shape: pltpu.VMEM(shape, F32)
    dma = lambda *shape: pltpu.SemaphoreType.DMA(shape)
    scratch = [
        vmem(*block), vmem(*framed), vmem(*block), vmem(*block),
        vmem(*framed), vmem(SWEEPS + 1, *framed), vmem(*block), vmem(*block),
        vmem(*block), vmem(*block),
        vmem(items, 2, depth, extent), vmem(items, 2, depth, extent),
        vmem(2, depth, extent), vmem(len(near), 2, 2, depth, extent),
        vmem(2, span, extent), vmem(2, 2, span, extent), vmem(2, *block),
        vmem(span, extent), vmem(span, extent), vmem(depth, extent),
        vmem(depth, span, extent + BX), pltpu.VMEM((2 * BX, BX), jnp.bfloat16),
        dma(4), dma(items, groups, 2), dma(items, groups, 2), dma(items, 2), dma(items, 2),
        dma(len(near), groups, 2), dma(len(near), groups, 2), dma(2), dma(2),
        dma(groups, 2), dma(groups, 2),
    ]
    if far:
        scratch += [
            vmem(len(far), 2, *block), dma(len(far), groups, 2), dma(len(far), groups, 2),
        ]
    return pl.pallas_call(
        functools.partial(kernel, n_grp, n_blk, near, far),
        out_shape=jax.ShapeDtypeStruct(block, F32),
        in_specs=[pl.BlockSpec(memory_space=pl.ANY)] * 4
        + [pl.BlockSpec(memory_space=pltpu.SMEM)],
        out_specs=pl.BlockSpec(memory_space=pltpu.VMEM),
        scratch_shapes=scratch,
        compiler_params=pltpu.CompilerParams(
            collective_id=0, has_side_effects=True, vmem_limit_bytes=60 * 2**20
        ),
        cost_estimate=pl.CostEstimate(
            flops=2 * 10**9, bytes_accessed=8 * 10**6, transcendentals=0
        ),
    )(solid, temp, target, coupling, switch)


def solution(mesh):
    spec = P("grp", "blk", None)
    return jax.shard_map(
        functools.partial(local, mesh.shape["grp"], mesh.shape["blk"]),
        mesh=mesh,
        in_specs=(spec,) * 5,
        out_specs=spec,
        check_vma=False,
    )
```

profile of v0, /device:TPU:1, one launch (start us, length us, event | category | flops | bytes accessed | tf_op | source)
XLA Modules:
  0.0 117.1 jit_solution(15381179138928929314)
XLA Ops:
  0.0 114.3 %shard_map.55 = f32[24,8,2048]{2,1,0:T(8,128)} custom-call(f32[24,8,2048]{2,1,0:T(8,128)} %refs_0_.1, f32[24,8,2048]{2,1,0:T(8,128)} %refs_1_.1, f32[24,8,2048]{2,1,0:T(8,128)} %refs_2_.1, f32[24,8,2048]{2,1,0:T(8,128)} %refs_3_.1, s32[1,1,8]{2,1,0:T(1,128)} %refs_4_.1), custom_call_target="tpu_custom_call" | custom-call | flops 2000000000 | bytes 8000000 | tf_op jit(solution)/shard_map/pallas_call | solution.py:482
  114.4 2.7 %copy.7 = f32[24,8,2048]{2,1,0:T(8,128)} copy(f32[24,8,2048]{2,1,0:T(8,128)} %shard_map.55) | data formatting | bytes 3145728
where the time goes:
time: 117 us
  Pallas kernels  114 us (97%)
  local copies, waits for them, and re-layouts  2.7 us (2%)
    pallas_call x1, Pallas kernels, local(): pl.pallas_call(functools.partial(kernel, n_grp, n_blk, near, far), out_sh...  114 us
    unnamed x1, local copies, waits for them, and re-layouts  2.7 us

commit v1 on v0

--- a/solution.py
+++ b/solution.py
@@ -34,7 +34,8 @@
         mask, scale, z_inv, padded, cone,
         load_sem, y_ssem, y_rsem, z_ssem, z_rsem,
         mom_ssem, mom_rsem, zm_ssem, zm_rsem, fz_ssem, fz_rsem,
-    ) = refs[:39]
+        passing, pass_ssem, pass_rsem, onward_ssem,
+    ) = refs[:43]
     depth, span, extent = solid.shape
     groups = depth // GROUP
     grp = lax.axis_index("grp")
@@ -105,7 +106,7 @@
 
             @pl.when(jnp.logical_not(has("blk", d * step)))
             def _(side=side, k=k):
-                refs[39][k, side] = jnp.zeros((depth, span, extent), F32)
+                refs[43][k, side] = jnp.zeros((depth, span, extent), F32)
 
     row = lax.broadcasted_iota(jnp.int32, (span, extent), 0)
     lane = lax.broadcasted_iota(jnp.int32, (span, extent), 1)
@@ -150,6 +151,55 @@
             "blk", 1 if side == 0 else -1,
         )
 
+    def by_corner(item, g):
+        return n_blk == 4 and (item == 1 or (item >= 2 and g == groups - 1))
+
+    def to_corner(item, g, side):
+        rows = pl.ds(g * GROUP, GROUP)
+        return remote(
+            y_send.at[item, side, rows], passing.at[item, rows],
+            pass_ssem.at[item, g], pass_rsem.at[item, g],
+            "blk", 2 if side == 0 else -2,
+        )
+
+    def from_corner(item, g, side):
+        rows = pl.ds(g * GROUP, GROUP)
+        return remote(
+            passing.at[item, rows], y_recv.at[item, side, rows],
+            onward_ssem.at[item, g], y_rsem.at[item, g, side],
+            "blk", -1 if side == 0 else 1,
+        )
+
+    def y_out(item, g, act):
+        for side, sign in ((0, 1), (1, -1)):
+            where = has("blk", sign)
+            if by_corner(item, g):
+                source = blk == (1 if side == 0 else 2)
+                where = jnp.logical_and(where, jnp.logical_not(source))
+
+                @pl.when(source)
+                def _(side=side):
+                    copy = to_corner(item, g, side)
+                    copy.start() if act == "start" else copy.wait_send()
+
+            @pl.when(where)
+            def _(side=side):
+                copy = y_copy(item, g, side)
+                copy.start() if act == "start" else copy.wait_send()
+
+    def corner(item, g, act):
+        if not by_corner(item, g):
+            return
+        for side, at in ((0, 3), (1, 0)):
+
+            @pl.when(blk == at)
+            def _(side=side):
+                if act == "start":
+                    to_corner(item, g, side).wait_recv()
+                    from_corner(item, g, side).start()
+                else:
+                    from_corner(item, g, side).wait_send()
+
     def z_copy(item, buf, side):
         src, dst = (depth, 0) if side == 0 else (1, depth + 1)
         return remote(
@@ -168,8 +218,8 @@
     def far_y_copy(k, g, side):
         rows = pl.ds(g * GROUP, GROUP)
         return remote(
-            raw.at[rows], refs[39].at[k, side, rows],
-            refs[40].at[k, g, side], refs[41].at[k, g, side],
+            raw.at[rows], refs[43].at[k, side, rows],
+            refs[44].at[k, g, side], refs[45].at[k, g, side],
             "blk", far[k] if side == 0 else -far[k],
         )
 
@@ -249,7 +299,7 @@
     pl.semaphore_wait(barrier, total)
     for g in range(groups):
         layers(g, conductivity)
-        both(functools.partial(y_copy, 0, g), "blk", 1, "start")
+        y_out(0, g, "start")
         if g == 0:
             one(functools.partial(z_copy, 0, cond), "grp", 1, 1, "start")
     one(functools.partial(z_copy, 0, cond), "grp", 1, 0, "start")
@@ -323,10 +373,15 @@
                 if wait_item == SWEEPS + 2:
                     one(functools.partial(z_copy, 1, temp), "grp", 1, 1, "come")
             layers(g, body)
+            if g == 0:
+                corner(wait_item, groups - 1, "start")
+                if wait_item == 3:
+                    for part in range(groups):
+                        corner(1, part, "start")
             if item is None:
                 after(g)
             else:
-                both(functools.partial(y_copy, item, g), "blk", 1, "start")
+                y_out(item, g, "start")
                 if g == 0:
                     one(functools.partial(z_copy, item, buf), "grp", 1, 1, "start")
         if item is not None:
@@ -334,7 +389,7 @@
 
     stage(2, adj.at[0], start_adjoint, 0, cond, None)
     for g in range(groups):
-        both(functools.partial(y_copy, 1, g), "blk", 1, "start")
+        y_out(1, g, "start")
     both(functools.partial(z_copy, 1, temp), "grp", 1, "start")
     for s in range(SWEEPS):
         stage(s + 3, adj.at[s + 1], functools.partial(sweep, s), s + 2, adj.at[s], None)
@@ -363,7 +418,7 @@
         for i in range(span):
             value = value + (RADIUS + 1 - jnp.abs(row - i)).astype(F32) * here[i : i + 1]
         for k, d in enumerate(far):
-            low, high = refs[39][k, 0, z], refs[39][k, 1, z]
+            low, high = refs[43][k, 0, z], refs[43][k, 1, z]
             for i in range(span):
                 w_low = jnp.maximum(RADIUS + 1 - (span * d + row - i), 0).astype(F32)
                 w_high = jnp.maximum(RADIUS + 1 - (span * d + i - row), 0).astype(F32)
@@ -435,7 +490,8 @@
 
     for item in range(SWEEPS + 3):
         for g in range(groups):
-            both(functools.partial(y_copy, item, g), "blk", 1, "sent")
+            y_out(item, g, "sent")
+            corner(item, g, "sent")
         buf = (cond, temp)[item] if item < 2 else adj.at[item - 2]
         both(functools.partial(z_copy, item, buf), "grp", 1, "sent")
     for g in range(groups):
@@ -474,6 +530,7 @@
         dma(4), dma(items, groups, 2), dma(items, groups, 2), dma(items, 2), dma(items, 2),
         dma(len(near), groups, 2), dma(len(near), groups, 2), dma(2), dma(2),
         dma(groups, 2), dma(groups, 2),
+        vmem(items, depth, extent), dma(items, groups), dma(items, groups), dma(items, groups),
     ]
     if far:
         scratch += [

time: 117 us -> 110 us (0.940)
  Pallas kernels: 114 us -> 107 us
    pallas_call x1, Pallas kernels: 114 us -> 107 us  [local(): pl.pallas_call(functools.partial(kernel, n_grp, n_blk, near, far), out_sh...]
where the time goes in v1:
time: 110 us
  Pallas kernels  107 us (97%)
  local copies, waits for them, and re-layouts  2.7 us (2%)
    pallas_call x1, Pallas kernels, local(): pl.pallas_call(functools.partial(kernel, n_grp, n_blk, near, far), out_sh...  107 us
    unnamed x1, local copies, waits for them, and re-layouts  2.7 us

profile of v1, /device:TPU:1, one launch (start us, length us, event | category | flops | bytes accessed | tf_op | source)
XLA Modules:
  0.0 109.7 jit_solution(12226554263056528372)
XLA Ops:
  0.0 107.0 %shard_map.55 = f32[24,8,2048]{2,1,0:T(8,128)} custom-call(f32[24,8,2048]{2,1,0:T(8,128)} %refs_0_.1, f32[24,8,2048]{2,1,0:T(8,128)} %refs_1_.1, f32[24,8,2048]{2,1,0:T(8,128)} %refs_2_.1, f32[24,8,2048]{2,1,0:T(8,128)} %refs_3_.1, s32[1,1,8]{2,1,0:T(1,128)} %refs_4_.1), custom_call_target="tpu_custom_call" | custom-call | flops 2000000000 | bytes 8000000 | tf_op jit(solution)/shard_map/pallas_call | solution.py:539
  107.0 2.7 %copy.7 = f32[24,8,2048]{2,1,0:T(8,128)} copy(f32[24,8,2048]{2,1,0:T(8,128)} %shard_map.55) | data formatting | bytes 3145728

commit v2 on v1

--- a/solution.py
+++ b/solution.py
@@ -28,14 +28,14 @@
 def kernel(n_grp, n_blk, near, far, *refs):
     (
         solid_hbm, temp_hbm, target_hbm, coupling_hbm, switch,
-        out,
+        padded,
         solid, temp, target, coupling, cond, adj, third, fixed, raw, filt,
         y_send, y_recv, mom_send, mom_recv, zmom_send, zmom_recv, far_z,
-        mask, scale, z_inv, padded, cone,
+        mask, scale, z_inv,
         load_sem, y_ssem, y_rsem, z_ssem, z_rsem,
         mom_ssem, mom_rsem, zm_ssem, zm_rsem, fz_ssem, fz_rsem,
         passing, pass_ssem, pass_rsem, onward_ssem,
-    ) = refs[:43]
+    ) = refs[:41]
     depth, span, extent = solid.shape
     groups = depth // GROUP
     grp = lax.axis_index("grp")
@@ -106,7 +106,7 @@
 
             @pl.when(jnp.logical_not(has("blk", d * step)))
             def _(side=side, k=k):
-                refs[43][k, side] = jnp.zeros((depth, span, extent), F32)
+                refs[41][k, side] = jnp.zeros((depth, span, extent), F32)
 
     row = lax.broadcasted_iota(jnp.int32, (span, extent), 0)
     lane = lax.broadcasted_iota(jnp.int32, (span, extent), 1)
@@ -124,16 +124,6 @@
     z_inv[...] = 1.0 / coverage(
         lax.broadcasted_iota(jnp.int32, (depth, extent), 0) + grp * depth, depth * n_grp
     )
-    cone[...] = jnp.maximum(
-        RADIUS
-        + 1
-        - jnp.abs(
-            lax.broadcasted_iota(jnp.int32, (2 * BX, BX), 0)
-            - BX // 2
-            - lax.broadcasted_iota(jnp.int32, (2 * BX, BX), 1)
-        ),
-        0,
-    ).astype(F32).astype(jnp.bfloat16)
     padded[:, :, : BX // 2] = jnp.zeros((depth, span, BX // 2), F32)
     padded[:, :, extent + BX // 2 :] = jnp.zeros((depth, span, BX // 2), F32)
 
@@ -152,7 +142,7 @@
         )
 
     def by_corner(item, g):
-        return n_blk == 4 and (item == 1 or (item >= 2 and g == groups - 1))
+        return n_blk == 4 and (item == 1 or g == groups - 1)
 
     def to_corner(item, g, side):
         rows = pl.ds(g * GROUP, GROUP)
@@ -218,8 +208,8 @@
     def far_y_copy(k, g, side):
         rows = pl.ds(g * GROUP, GROUP)
         return remote(
-            raw.at[rows], refs[43].at[k, side, rows],
-            refs[44].at[k, g, side], refs[45].at[k, g, side],
+            raw.at[rows], refs[41].at[k, side, rows],
+            refs[42].at[k, g, side], refs[43].at[k, g, side],
             "blk", far[k] if side == 0 else -far[k],
         )
 
@@ -418,7 +408,7 @@
         for i in range(span):
             value = value + (RADIUS + 1 - jnp.abs(row - i)).astype(F32) * here[i : i + 1]
         for k, d in enumerate(far):
-            low, high = refs[43][k, 0, z], refs[43][k, 1, z]
+            low, high = refs[41][k, 0, z], refs[41][k, 1, z]
             for i in range(span):
                 w_low = jnp.maximum(RADIUS + 1 - (span * d + row - i), 0).astype(F32)
                 w_high = jnp.maximum(RADIUS + 1 - (span * d + i - row), 0).astype(F32)
@@ -472,21 +462,6 @@
             return far_twice, far_once
 
         lax.fori_loop(0, depth, down, (zero, zero))
-
-    @pl.loop(0, extent // BX)
-    def _(b):
-        window = padded[:, :, pl.ds(pl.multiple_of(b * BX, BX), 2 * BX)]
-        window = window.reshape(depth * span, 2 * BX)
-        high = window.astype(jnp.bfloat16)
-        low = (window - high.astype(F32)).astype(jnp.bfloat16)
-        weights = cone[...]
-        product = jnp.dot(high, weights, preferred_element_type=F32) + jnp.dot(
-            low, weights, preferred_element_type=F32
-        )
-        cols = pl.ds(pl.multiple_of(b * BX, BX), BX)
-        out[:, :, cols] = product.reshape(depth, span, BX) * (
-            REPORT_SCALE * mask[:, cols]
-        )
 
     for item in range(SWEEPS + 3):
         for g in range(groups):
@@ -501,6 +476,33 @@
             both(functools.partial(far_y_copy, k, g), "blk", d, "sent")
         both(functools.partial(far_z_copy, g), "grp", 2, "sent")
     both(zmom_copy, "grp", 1, "sent")
+
+
+def along_x(switch, padded, out, cone):
+    depth, span, _ = out.shape
+    b = pl.program_id(0)
+
+    @pl.when(b == 0)
+    def _():
+        distance = (
+            lax.broadcasted_iota(jnp.int32, (2 * BX, BX), 0)
+            - BX // 2
+            - lax.broadcasted_iota(jnp.int32, (2 * BX, BX), 1)
+        )
+        weights = jnp.maximum(RADIUS + 1 - jnp.abs(distance), 0)
+        cone[...] = weights.astype(F32).astype(jnp.bfloat16)
+
+    window = padded[:, :, pl.ds(pl.multiple_of(b * BX, BX), 2 * BX)]
+    window = window.reshape(depth * span, 2 * BX)
+    high = window.astype(jnp.bfloat16)
+    low = (window - high.astype(F32)).astype(jnp.bfloat16)
+    weights = cone[...]
+    product = jnp.dot(high, weights, preferred_element_type=F32) + jnp.dot(
+        low, weights, preferred_element_type=F32
+    )
+    out[...] = product.reshape(depth, span, BX) * (
+        REPORT_SCALE * switch[0, 0, b].astype(F32)
+    )
 
 
 def local(n_grp, n_blk, solid, temp, target, coupling, switch):
@@ -526,7 +528,6 @@
         vmem(2, depth, extent), vmem(len(near), 2, 2, depth, extent),
         vmem(2, span, extent), vmem(2, 2, span, extent), vmem(2, *block),
         vmem(span, extent), vmem(span, extent), vmem(depth, extent),
-        vmem(depth, span, extent + BX), pltpu.VMEM((2 * BX, BX), jnp.bfloat16),
         dma(4), dma(items, groups, 2), dma(items, groups, 2), dma(items, 2), dma(items, 2),
         dma(len(near), groups, 2), dma(len(near), groups, 2), dma(2), dma(2),
         dma(groups, 2), dma(groups, 2),
@@ -536,9 +537,9 @@
         scratch += [
             vmem(len(far), 2, *block), dma(len(far), groups, 2), dma(len(far), groups, 2),
         ]
-    return pl.pallas_call(
+    padded = pl.pallas_call(
         functools.partial(kernel, n_grp, n_blk, near, far),
-        out_shape=jax.ShapeDtypeStruct(block, F32),
+        out_shape=jax.ShapeDtypeStruct((depth, span, extent + BX), F32),
         in_specs=[pl.BlockSpec(memory_space=pl.ANY)] * 4
         + [pl.BlockSpec(memory_space=pltpu.SMEM)],
         out_specs=pl.BlockSpec(memory_space=pltpu.VMEM),
@@ -550,6 +551,18 @@
             flops=2 * 10**9, bytes_accessed=8 * 10**6, transcendentals=0
         ),
     )(solid, temp, target, coupling, switch)
+    return pl.pallas_call(
+        along_x,
+        out_shape=jax.ShapeDtypeStruct(block, F32),
+        grid=(extent // BX,),
+        in_specs=[
+            pl.BlockSpec(memory_space=pltpu.SMEM),
+            pl.BlockSpec((depth, span, extent + BX), lambda b: (0, 0, 0)),
+        ],
+        out_specs=pl.BlockSpec((depth, span, BX), lambda b: (0, 0, b)),
+        scratch_shapes=[pltpu.VMEM((2 * BX, BX), jnp.bfloat16)],
+        compiler_params=pltpu.CompilerParams(vmem_limit_bytes=24 * 2**20),
+    )(switch, padded)
 
 
 def solution(mesh):

time: 110 us -> 110 us (level)
  local copies, waits for them, and re-layouts: 2.7 us -> 1.47 us
    pallas_call x0 -> x1, Pallas kernels: none -> 4.84 us  [local(): pl.pallas_call(along_x, out_shape=jax.ShapeDtypeStruct(block, F32), grid=...]
    pallas_call x1, Pallas kernels: 107 us -> 104 us  [local(): pl.pallas_call(functools.partial(kernel, n_grp, n_blk, near, far), out_sh...]
    unnamed x1 -> x4, local copies, waits for them, and re-layouts: 2.7 us -> 1.47 us
where the time goes in v2:
time: 110 us
  Pallas kernels  108 us (98%)
  local copies, waits for them, and re-layouts  1.47 us (1%)
    pallas_call x1, Pallas kernels, local(): pl.pallas_call(functools.partial(kernel, n_grp, n_blk, near, far), out_sh...  104 us
    pallas_call x1, Pallas kernels, local(): pl.pallas_call(along_x, out_shape=jax.ShapeDtypeStruct(block, F32), grid=...  4.84 us

profile of v2, /device:TPU:1, one launch (start us, length us, event | category | flops | bytes accessed | tf_op | source)
XLA Modules:
  0.0 109.9 jit_solution(6966015949528092366)
XLA Ops:
  0.0 0.0 copy-start.1
  0.0 103.6 %shard_map.55.padded = f32[24,8,2304]{2,1,0:T(8,128)} custom-call(f32[24,8,2048]{2,1,0:T(8,128)} %refs_0_.1, f32[24,8,2048]{2,1,0:T(8,128)} %refs_1_.1, f32[24,8,2048]{2,1,0:T(8,128)} %refs_2_.1, f32[24,8,2048]{2,1,0:T(8,128)} %refs_3_.1, s32[1,1,8]{2,1,0:T(1,128)} %switch.1), custom_call_target="tpu_custom_call" | custom-call | flops 2000000000 | bytes 8000000 | tf_op jit(solution)/shard_map/pallas_call | solution.py:540
  103.6 0.0 copy-done.1
  103.6 0.0 copy-start
  103.6 1.5 %copy-done = f32[24,8,2304]{2,1,0:T(8,128)S(1)} copy-done((f32[24,8,2304]{2,1,0:T(8,128)S(1)}, f32[24,8,2304]{2,1,0:T(8,128)}, u32[]{:S(2)}) %copy-start) | copy-done | bytes 1769496
  105.1 4.8 %shard_map.56 = f32[24,8,2048]{2,1,0:T(8,128)} custom-call(s32[1,1,8]{2,1,0:T(1,128)S(1)} %copy-done.1, f32[24,8,2304]{2,1,0:T(8,128)S(1)} %copy-done), custom_call_target="tpu_custom_call" | custom-call | tf_op jit(solution)/shard_map/pallas_call | solution.py:554
Async XLA Ops:
  0.0 103.6 %copy-start.1 = (s32[1,1,8]{2,1,0:T(1,128)S(1)}, s32[1,1,8]{2,1,0:T(1,128)}, u32[]{:S(2)}) copy-start(s32[1,1,8]{2,1,0:T(1,128)} %switch.1) | copy-start | bytes 100
  103.6 1.5 %copy-start = (f32[24,8,2304]{2,1,0:T(8,128)S(1)}, f32[24,8,2304]{2,1,0:T(8,128)}, u32[]{:S(2)}) copy-start(f32[24,8,2304]{2,1,0:T(8,128)} %shard_map.55.padded) | copy-start | bytes 5308420
